TPU v7x, 32 devices: a whole 2x2x4 slice. The times are simulated.
32 devices in a mesh: shard: 8 (over y, x, core), rep: 4 (over z).
Axes of the slice: x: 2, y: 2, z: 4, core: 2. Of those that a mesh axis runs over, the one named last changes fastest.
Arguments:
- tokens: bfloat16 [32768, 768], P(('shard', 'rep')), may hold values from -6 to 6
- segments: int32 [32768], P(('shard', 'rep')), may hold values from -1 to 1023, as said below
- cotangent: bfloat16 [32768, 768], P(('shard', 'rep')), may hold values from -6 to 6
- attend_gain: bfloat16 [768], P('shard'), may hold values from 0.099609375 to 1.8984375
- attend_shift: bfloat16 [768], P('shard'), may hold values from -2 to 2
- triple_weight: bfloat16 [768, 2304], P('shard'), may hold values from -0.21875 to 0.21875
- triple_bias: bfloat16 [1536], P('shard'), may hold values from -2 to 2
- output_weight: bfloat16 [768, 768], P('shard'), may hold values from -0.875 to 0.875
- output_bias: bfloat16 [768], P('shard'), may hold values from -2 to 2
- feed_gain: bfloat16 [768], P('shard'), may hold values from 0.099609375 to 1.8984375
- feed_shift: bfloat16 [768], P('shard'), may hold values from -2 to 2
- expand_weight: bfloat16 [768, 3072], P('shard'), may hold values from -0.21875 to 0.21875
- expand_bias: bfloat16 [3072], P('shard'), may hold values from -2 to 2
- reduce_weight: bfloat16 [3072, 768], P('shard'), may hold values from -0.109375 to 0.109375
- reduce_bias: bfloat16 [768], P('shard'), may hold values from -2 to 2
Outputs:
- out_tokens: bfloat16 [32768, 768], P(('shard', 'rep'))
- grad_tokens: bfloat16 [32768, 768], P(('shard', 'rep'))
- grad_attend_gain: float32 [768], P('shard')
- grad_attend_shift: float32 [768], P('shard')
- grad_triple_weight: float32 [768, 2304], P('shard')
- grad_triple_bias: float32 [1536], P('shard')
- grad_output_weight: float32 [768, 768], P('shard')
- grad_output_bias: float32 [768], P('shard')
- grad_feed_gain: float32 [768], P('shard')
- grad_feed_shift: float32 [768], P('shard')
- grad_expand_weight: float32 [768, 3072], P('shard')
- grad_expand_bias: float32 [3072], P('shard')
- grad_reduce_weight: float32 [3072, 768], P('shard')
- grad_reduce_bias: float32 [768], P('shard')
Inputs may be any that keep to these rules, and one draw needn't show every extreme that they name: `segments`: within the 1024 slots of one device, numbers never fall along the slots, start at 0 and rise by at most one from slot to slot; empty slots (-1) come after all live slots of that device; each document has at most 1024 tokens; some device holds a single document of 1024 tokens, some device holds 1024 documents of one token, and some device has empty slots; every device has 256 live slots or more.
All inputs are finite; a program needn't handle non-finite values.
Results may differ from a plain program's by a relative error of at most 0.018.
Values may be sent and summed in bfloat16 or wider, within the bound.
No kernel may reach another device: no remote copies, remote signals or barrier semaphores. Data moves between devices by JAX's collectives and lax.ppermute only.
A program may use at most 256 MiB of HBM per device.

v0:
```python
import jax
import jax.numpy as jnp
from jax import lax
from jax.sharding import PartitionSpec as P

D = 768
HEADS = 12
HEAD_DIM = 64


epsilon = 1e-05


def layer_norm(values, gain, shift):
    center = values - jnp.mean(values, axis=-1, keepdims=True)
    variance = jnp.mean(center * center, axis=-1, keepdims=True)
    return center * lax.rsqrt(variance + epsilon) * gain + shift


def dot_float(left, right):
    return jnp.dot(left, right, preferred_element_type=jnp.float32)


def allowed_block(segments, start, block):
    rows = segments.shape[0]
    seg_part = lax.dynamic_slice_in_dim(segments, start, block, 0)
    query_pos = start + jnp.arange(block)
    return (seg_part[:, None] == segments[None, :]) & (
        jnp.arange(rows)[None, :] <= query_pos[:, None]
    )


def attend_forward(queries, keys, values, segments, block):
    rows = queries.shape[0]

    def one_block(start):
        query_part = lax.dynamic_slice_in_dim(queries, start, block, 0)
        allowed = allowed_block(segments, start, block)
        scores = (
            jnp.einsum("qhd,khd->hqk", query_part, keys, preferred_element_type=jnp.float32) * 0.125
        )
        masked = jnp.where(allowed[None], scores, -1000000000.0)
        largest = jnp.max(masked, axis=-1, keepdims=True)
        expo = jnp.exp(masked - largest)
        totals = jnp.sum(expo, axis=-1, keepdims=True)
        weights = (expo / totals).astype(jnp.bfloat16)
        mixed = jnp.einsum("hqk,khd->qhd", weights, values, preferred_element_type=jnp.float32)
        return (mixed.astype(jnp.bfloat16), (largest + jnp.log(totals))[..., 0])

    starts = jnp.arange(rows // block, dtype=jnp.int32) * block
    mixed, log_total = lax.map(one_block, starts)
    return (mixed.reshape(rows, -1), log_total)


def attend_backward(queries, keys, values, segments, log_total, mixed_grad, block):
    rows = queries.shape[0]
    starts = jnp.arange(rows // block, dtype=jnp.int32) * block

    def one_block(carry, item):
        start, log_part = item
        key_total, value_total = carry
        query_part = lax.dynamic_slice_in_dim(queries, start, block, 0)
        grad_part = lax.dynamic_slice_in_dim(mixed_grad, start, block, 0)
        allowed = allowed_block(segments, start, block)
        scores = (
            jnp.einsum("qhd,khd->hqk", query_part, keys, preferred_element_type=jnp.float32) * 0.125
        )
        probs = jnp.where(allowed[None], jnp.exp(scores - log_part[..., None]), 0.0)
        prob_grad = jnp.einsum(
            "qhd,khd->hqk", grad_part, values, preferred_element_type=jnp.float32
        )
        inner = jnp.sum(probs * prob_grad, axis=-1, keepdims=True)
        score_grad = (probs * (prob_grad - inner)).astype(jnp.bfloat16)
        query_grad = (
            jnp.einsum("hqk,khd->qhd", score_grad, keys, preferred_element_type=jnp.float32) * 0.125
        )
        key_total = (
            key_total
            + jnp.einsum("hqk,qhd->khd", score_grad, query_part, preferred_element_type=jnp.float32)
            * 0.125
        )
        value_total = value_total + jnp.einsum(
            "hqk,qhd->khd",
            probs.astype(jnp.bfloat16),
            grad_part,
            preferred_element_type=jnp.float32,
        )
        return ((key_total, value_total), query_grad)

    empty = jnp.zeros(keys.shape, jnp.float32)
    (key_grad, value_grad), query_grad = lax.scan(one_block, (empty, empty), (starts, log_total))
    return (query_grad.reshape(keys.shape), key_grad, value_grad)


def shards(
    tokens,
    segments,
    cotangent,
    attend_gain,
    attend_shift,
    triple_weight,
    triple_bias,
    output_weight,
    output_bias,
    feed_gain,
    feed_shift,
    expand_weight,
    expand_bias,
    reduce_weight,
    reduce_bias,
):
    whole = (
        lax.all_gather(attend_gain, "shard", axis=0, tiled=True),
        lax.all_gather(attend_shift, "shard", axis=0, tiled=True),
        lax.all_gather(triple_weight, "shard", axis=0, tiled=True),
        lax.all_gather(triple_bias, "shard", axis=0, tiled=True),
        lax.all_gather(output_weight, "shard", axis=0, tiled=True),
        lax.all_gather(output_bias, "shard", axis=0, tiled=True),
        lax.all_gather(feed_gain, "shard", axis=0, tiled=True),
        lax.all_gather(feed_shift, "shard", axis=0, tiled=True),
        lax.all_gather(expand_weight, "shard", axis=0, tiled=True),
        lax.all_gather(expand_bias, "shard", axis=0, tiled=True),
        lax.all_gather(reduce_weight, "shard", axis=0, tiled=True),
        lax.all_gather(reduce_bias, "shard", axis=0, tiled=True),
    )
    gain_one = whole[0].astype(jnp.float32)
    shift_one = whole[1].astype(jnp.float32)
    triple_shift = whole[3].astype(jnp.float32)
    output_shift = whole[5].astype(jnp.float32)
    gain_two = whole[6].astype(jnp.float32)
    shift_two = whole[7].astype(jnp.float32)
    expand_shift = whole[9].astype(jnp.float32)
    reduce_shift = whole[11].astype(jnp.float32)
    rows = tokens.shape[0]
    block = min(512, rows)
    inputs = tokens.astype(jnp.float32)
    live_rows = (segments >= 0).astype(jnp.float32)[:, None]
    normed = layer_norm(inputs, gain_one, shift_one).astype(jnp.bfloat16)
    bias_full = jnp.concatenate([triple_shift[:D], jnp.zeros((D,), jnp.float32), triple_shift[D:]])
    projected = (dot_float(normed, whole[2]) + bias_full).astype(jnp.bfloat16)
    queries = projected[:, :D].reshape(rows, HEADS, HEAD_DIM)
    keys = projected[:, D : 2 * D].reshape(rows, HEADS, HEAD_DIM)
    values = projected[:, 2 * D :].reshape(rows, HEADS, HEAD_DIM)
    mixed, log_total = attend_forward(queries, keys, values, segments, block)
    middle = inputs + dot_float(mixed, whole[4]) + output_shift
    normed_two = layer_norm(middle, gain_two, shift_two).astype(jnp.bfloat16)
    expanded = dot_float(normed_two, whole[8]) + expand_shift
    hidden = jax.nn.gelu(expanded).astype(jnp.bfloat16)
    result = live_rows * (middle + dot_float(hidden, whole[10]) + reduce_shift)
    out_tokens = result.astype(jnp.bfloat16)
    again = (
        lax.all_gather(attend_gain, "shard", axis=0, tiled=True),
        lax.all_gather(triple_weight, "shard", axis=0, tiled=True),
        lax.all_gather(output_weight, "shard", axis=0, tiled=True),
        lax.all_gather(feed_gain, "shard", axis=0, tiled=True),
        lax.all_gather(expand_weight, "shard", axis=0, tiled=True),
        lax.all_gather(reduce_weight, "shard", axis=0, tiled=True),
    )
    back_gain_one = again[0].astype(jnp.float32)
    back_gain_two = again[3].astype(jnp.float32)
    zero_shift = jnp.zeros((D,), jnp.float32)
    grad_out = live_rows * cotangent.astype(jnp.float32)
    feed_grad = grad_out.astype(jnp.bfloat16)
    grad_reduce_bias = jnp.sum(feed_grad.astype(jnp.float32), axis=0)
    grad_reduce_weight = jnp.einsum(
        "tf,td->fd", hidden, feed_grad, preferred_element_type=jnp.float32
    )
    hidden_grad = jnp.einsum("td,fd->tf", feed_grad, again[5], preferred_element_type=jnp.float32)
    _, gelu_back = jax.vjp(jax.nn.gelu, expanded)
    expand_grad = gelu_back(hidden_grad)[0].astype(jnp.bfloat16)
    grad_expand_bias = jnp.sum(expand_grad.astype(jnp.float32), axis=0)
    grad_expand_weight = jnp.einsum(
        "td,tf->df", normed_two, expand_grad, preferred_element_type=jnp.float32
    )
    normed_two_grad = jnp.einsum(
        "tf,df->td", expand_grad, again[4], preferred_element_type=jnp.float32
    )
    _, norm_back_two = jax.vjp(
        lambda rows_in, gain: layer_norm(rows_in, gain, zero_shift), middle, back_gain_two
    )
    middle_part, grad_feed_gain = norm_back_two(normed_two_grad)
    grad_feed_shift = jnp.sum(normed_two_grad, axis=0)
    grad_middle = grad_out + middle_part
    branch_grad = grad_middle.astype(jnp.bfloat16)
    grad_output_bias = jnp.sum(branch_grad.astype(jnp.float32), axis=0)
    grad_output_weight = jnp.einsum(
        "td,te->de", mixed, branch_grad, preferred_element_type=jnp.float32
    )
    mixed_grad = jnp.einsum("te,de->td", branch_grad, again[2], preferred_element_type=jnp.float32)
    mixed_grad = mixed_grad.astype(jnp.bfloat16).reshape(rows, HEADS, HEAD_DIM)
    query_grad, key_grad, value_grad = attend_backward(
        queries, keys, values, segments, log_total, mixed_grad, block
    )
    projected_grad = jnp.concatenate(
        [query_grad.reshape(rows, D), key_grad.reshape(rows, D), value_grad.reshape(rows, D)],
        axis=1,
    ).astype(jnp.bfloat16)
    column_sums = jnp.sum(projected_grad.astype(jnp.float32), axis=0)
    grad_triple_bias = jnp.concatenate([column_sums[:D], column_sums[2 * D :]])
    grad_triple_weight = jnp.einsum(
        "td,te->de", normed, projected_grad, preferred_element_type=jnp.float32
    )
    normed_grad = jnp.einsum(
        "te,de->td", projected_grad, again[1], preferred_element_type=jnp.float32
    )
    _, norm_back_one = jax.vjp(
        lambda rows_in, gain: layer_norm(rows_in, gain, zero_shift), inputs, back_gain_one
    )
    input_part, grad_attend_gain = norm_back_one(normed_grad)
    grad_attend_shift = jnp.sum(normed_grad, axis=0)
    grad_tokens = (grad_middle + input_part).astype(jnp.bfloat16)
    owned = (
        lax.psum_scatter(
            grad_attend_gain.astype(jnp.bfloat16), "shard", scatter_dimension=0, tiled=True
        ).astype(jnp.float32),
        lax.psum_scatter(
            grad_attend_shift.astype(jnp.bfloat16), "shard", scatter_dimension=0, tiled=True
        ).astype(jnp.float32),
        lax.psum_scatter(
            grad_triple_weight.astype(jnp.bfloat16), "shard", scatter_dimension=0, tiled=True
        ).astype(jnp.float32),
        lax.psum_scatter(
            grad_triple_bias.astype(jnp.bfloat16), "shard", scatter_dimension=0, tiled=True
        ).astype(jnp.float32),
        lax.psum_scatter(
            grad_output_weight.astype(jnp.bfloat16), "shard", scatter_dimension=0, tiled=True
        ).astype(jnp.float32),
        lax.psum_scatter(
            grad_output_bias.astype(jnp.bfloat16), "shard", scatter_dimension=0, tiled=True
        ).astype(jnp.float32),
        lax.psum_scatter(
            grad_feed_gain.astype(jnp.bfloat16), "shard", scatter_dimension=0, tiled=True
        ).astype(jnp.float32),
        lax.psum_scatter(
            grad_feed_shift.astype(jnp.bfloat16), "shard", scatter_dimension=0, tiled=True
        ).astype(jnp.float32),
        lax.psum_scatter(
            grad_expand_weight.astype(jnp.bfloat16), "shard", scatter_dimension=0, tiled=True
        ).astype(jnp.float32),
        lax.psum_scatter(
            grad_expand_bias.astype(jnp.bfloat16), "shard", scatter_dimension=0, tiled=True
        ).astype(jnp.float32),
        lax.psum_scatter(
            grad_reduce_weight.astype(jnp.bfloat16), "shard", scatter_dimension=0, tiled=True
        ).astype(jnp.float32),
        lax.psum_scatter(
            grad_reduce_bias.astype(jnp.bfloat16), "shard", scatter_dimension=0, tiled=True
        ).astype(jnp.float32),
    )
    owned = (
        lax.psum(owned[0].astype(jnp.bfloat16), "rep").astype(jnp.float32),
        lax.psum(owned[1].astype(jnp.bfloat16), "rep").astype(jnp.float32),
        lax.psum(owned[2].astype(jnp.bfloat16), "rep").astype(jnp.float32),
        lax.psum(owned[3].astype(jnp.bfloat16), "rep").astype(jnp.float32),
        lax.psum(owned[4].astype(jnp.bfloat16), "rep").astype(jnp.float32),
        lax.psum(owned[5].astype(jnp.bfloat16), "rep").astype(jnp.float32),
        lax.psum(owned[6].astype(jnp.bfloat16), "rep").astype(jnp.float32),
        lax.psum(owned[7].astype(jnp.bfloat16), "rep").astype(jnp.float32),
        lax.psum(owned[8].astype(jnp.bfloat16), "rep").astype(jnp.float32),
        lax.psum(owned[9].astype(jnp.bfloat16), "rep").astype(jnp.float32),
        lax.psum(owned[10].astype(jnp.bfloat16), "rep").astype(jnp.float32),
        lax.psum(owned[11].astype(jnp.bfloat16), "rep").astype(jnp.float32),
    )
    return (
        out_tokens,
        grad_tokens,
        owned[0],
        owned[1],
        owned[2],
        owned[3],
        owned[4],
        owned[5],
        owned[6],
        owned[7],
        owned[8],
        owned[9],
        owned[10],
        owned[11],
    )


def solution(mesh):
    return jax.shard_map(
        shards,
        mesh=mesh,
        in_specs=(
            P(("shard", "rep"), None),
            P(("shard", "rep")),
            P(("shard", "rep"), None),
            P("shard"),
            P("shard"),
            P("shard", None),
            P("shard"),
            P("shard", None),
            P("shard"),
            P("shard"),
            P("shard"),
            P("shard", None),
            P("shard"),
            P("shard", None),
            P("shard"),
        ),
        out_specs=(
            P(("shard", "rep"), None),
            P(("shard", "rep"), None),
            P("shard"),
            P("shard"),
            P("shard", None),
            P("shard"),
            P("shard", None),
            P("shard"),
            P("shard"),
            P("shard"),
            P("shard", None),
            P("shard"),
            P("shard", None),
            P("shard"),
        ),
        check_vma=False,
    )
```

profile of v0, /device:TPU:0, one launch (start us, length us, event | category | flops | bytes accessed | tf_op | source)
XLA Modules:
  0.0 667.8 jit_solution(14605078946544472011)
XLA Ops:
  19.7 26.0 %all-reduce.16 = (bf16[1536]{0:T(1024)(128)(2,1)S(1)}, bf16[768]{0:T(1024)(128)(2,1)S(1)}, bf16[768]{0:T(1024)(128)(2,1)S(1)}, bf16[768]{0:T(1024)(128)(2,1)S(1)...) all-reduce(bf16[1536]{0:T(1024)(128)(2,1)S(1)} %dynamic-update-slic, ...), channel_id=1, replica_groups=mesh['shard'=8,'rep'=4] {'shard'}, use_global_device_ids=true, to_apply=%add.2 | all-reduce | flops 5376 | bytes 21504
  72.4 79.7 %while.27 = (s32[]{:T(128)}, bf16[2,512,12,64]{1,3,2,0:T(8,128)(2,1)}, f32[2,12,512]{2,1,0:T(8,128)S(1)}, s32[2]{0:T(128)S(1)}, s32[1024]{0:T(1024)S(1)}, /*inde...) while((s32[]{:T(128)}, ...), condition=%wide.region_5.6_spmd, body=%wide.region_2.5_spmd.sunk | while | flops 1688070656 | bytes 189503728 | solution.py:51
  76.3 11.2 %fusion.115 = (f32[12,512]{1,0:T(8,128)S(1)}, f32[12,512,1024]{2,1,0:T(8,128)}) fusion(pred[512,1024]{1,0:T(8,128)(4,1)S(1)} %fusion.114, bf16[1024,12,64]{0,2,1:T(8,128)(2,1)S(1)} %get-tuple-element.465, bf16[1024,12,64]{0,2,1:T(8,128)(2,1)S(1)} %get-tuple-element.464, s32[]{:T(128)S(6)} %select_n.55), kind=kOutput, calls=%fused_computation.3.clone.1 | convolution fusion | flops 824174592 | bytes 28073988 | tf_op jit(solution)/shard_map/while/body/eval_jaxpr/qhd,khd->hqk/dot_general | solution.py:40
  87.4 13.1 %fusion.116 = f32[12,512]{1,0:T(8,128)S(1)} fusion(f32[12,512,1024]{2,1,0:T(8,128)} %get-tuple-element.422, f32[12,512]{1,0:T(8,128)S(1)} %get-tuple-element.423, pred[512,1024]{1,0:T(8,128)(4,1)S(1)} %fusion.114), kind=kLoop, calls=%fused_computation.4.clone.1 | loop fusion | flops 25159680 | bytes 25739264 | tf_op jit(solution)/shard_map/while/body/eval_jaxpr/reduce_sum | solution.py:45
  116.0 11.2 %fusion.115 = (f32[12,512]{1,0:T(8,128)S(1)}, f32[12,512,1024]{2,1,0:T(8,128)}) fusion(pred[512,1024]{1,0:T(8,128)(4,1)S(1)} %fusion.114, bf16[1024,12,64]{0,2,1:T(8,128)(2,1)S(1)} %get-tuple-element.465, bf16[1024,12,64]{0,2,1:T(8,128)(2,1)S(1)} %get-tuple-element.464, s32[]{:T(128)S(6)} %select_n.55), kind=kOutput, calls=%fused_computation.3.clone.1 | convolution fusion | flops 824174592 | bytes 28073988 | tf_op jit(solution)/shard_map/while/body/eval_jaxpr/qhd,khd->hqk/dot_general | solution.py:40
  127.2 12.3 %fusion.116 = f32[12,512]{1,0:T(8,128)S(1)} fusion(f32[12,512,1024]{2,1,0:T(8,128)} %get-tuple-element.422, f32[12,512]{1,0:T(8,128)S(1)} %get-tuple-element.423, pred[512,1024]{1,0:T(8,128)(4,1)S(1)} %fusion.114), kind=kLoop, calls=%fused_computation.4.clone.1 | loop fusion | flops 25159680 | bytes 25739264 | tf_op jit(solution)/shard_map/while/body/eval_jaxpr/reduce_sum | solution.py:45
  162.8 11.0 %fusion.62 = f32[1024,3072]{1,0:T(8,128)} fusion(bf16[768,3072]{1,0:T(8,128)(2,1)} %all-gather.10.cloned.1.call-done, f32[1024,768]{0,1:T(8,128)} %copy-done.7, f32[768]{0:T(1024)S(1)} %copy-done.30, f32[768]{0:T(1024)S(1)} %copy-done.26, f32[1024]{0:T(1024)S(1)} %fusion.57, f32[1024]{0:T(1024)S(1)} %broadcast_multiply_fusion), kind=kOutput, calls=%fused_computation.105 | convolution fusion | flops 4835770368 | bytes 20461568 | tf_op jit(solution)/shard_map/dot_general | solution.py:21
  173.9 17.8 %fusion.73 = (bf16[3072]{0:T(1024)(128)(2,1)}, bf16[1024,3072]{1,0:T(8,128)(2,1)S(1)}) fusion(f32[1024,3072]{1,0:T(8,128)} %fusion.62, f32[3072]{0:T(1024)S(1)} %bitcast.108, bf16[3072,768]{1,0:T(8,128)(2,1)} %all-gather.12.cloned.1.call-done, bf16[1024,768]{0,1:T(8,128)(2,1)} %copy.64, f32[1024]{0:T(1024)S(1)} %copy-done.40), kind=kOutput, calls=%fused_computation.115 | convolution fusion | flops 4903400448 | bytes 25188352 | tf_op jit(solution)/shard_map/td,fd->tf/dot_general | solution.py:168
  218.0 178.2 %while.28 = (s32[]{:T(128)}, f32[1024,12,64]{0,2,1:T(8,128)}, f32[1024,12,64]{0,2,1:T(8,128)}, bf16[2,512,12,64]{1,3,2,0:T(8,128)(2,1)}, s32[2]{0:T(128)S(1)}, /...) while((s32[]{:T(128)}, f32[1024,12,64]{0,2,1:T(8,128)}, ...), condition=%wide.region_12.13_spmd.clone, body=%wide.region_10.12_spmd.clone.sunk | while | flops 4126796288 | bytes 231930176 | solution.py:91
  222.2 13.5 %fusion.127 = f32[12,512,1024]{2,1,0:T(8,128)} fusion(bf16[1024,12,64]{0,2,1:T(8,128)(2,1)S(1)} %get-tuple-element.505, bf16[1024,12,64]{0,2,1:T(8,128)(2,1)} %copy-done.2, s32[]{:T(128)S(6)} %select_n.59), kind=kOutput, calls=%fused_computation.33.clone.1 | convolution fusion | flops 805306368 | bytes 27525124 | tf_op jit(solution)/shard_map/while/body/eval_jaxpr/qhd,khd->hqk/dot_general | solution.py:66
  235.7 13.1 %bitcast_add_fusion.5 = f32[1024,12,64]{0,2,1:T(8,128)} fusion(f32[1024,12,64]{0,2,1:T(8,128)} %get-tuple-element.486, f32[12,512,1024]{2,1,0:T(8,128)} %fusion.127, f32[12,512]{1,0:T(8,128)S(1)} %dynamic-slice_bitcast_fusion.2, pred[512,1024]{1,0:T(8,128)(4,1)S(1)} %fusion.128, pred[]{:T(512)S(6)} %compare.3, ...), kind=kOutput, calls=%fused_computation.24.clone.1 | convolution fusion | flops 832045056 | bytes 32800772 | tf_op jit(solution)/shard_map/while/body/eval_jaxpr/hqk,qhd->khd/dot_general | solution.py:82
  248.8 18.4 %multiply_reduce_fusion.5 = (f32[12,512]{1,0:T(8,128)S(1)}, f32[12,512,1024]{2,1,0:T(8,128)}) fusion(f32[12,512,1024]{2,1,0:T(8,128)} %fusion.127, f32[12,512]{1,0:T(8,128)S(1)} %dynamic-slice_bitcast_fusion.2, pred[512,1024]{1,0:T(8,128)(4,1)S(1)} %fusion.128, bf16[1024,12,64]{0,2,1:T(8,128)(2,1)} %get-tuple-element.508, ...), kind=kOutput, calls=%fused_computation.19.clone.1 | convolution fusion | flops 836757504 | bytes 53264388 | tf_op jit(solution)/shard_map/while/body/eval_jaxpr/qhd,khd->hqk/dot_general | solution.py:69
  267.1 21.1 %multiply_convert_fusion.6 = bf16[12,512,1024]{2,1,0:T(8,128)(2,1)} fusion(f32[12,512,1024]{2,1,0:T(8,128)} %get-tuple-element.435, f32[12,512,1024]{2,1,0:T(8,128)} %fusion.127, f32[12,512]{1,0:T(8,128)S(1)} %get-tuple-element.436, f32[12,512]{1,0:T(8,128)S(1)} %dynamic-slice_bitcast_fusion.2, pred[512,1024]{1,0:T(8,128)(4,1)S(1)} %fusion.128), kind=kLoop, calls=%fused_computation.18.clone.1 | loop fusion | flops 37748736 | bytes 63488000 | tf_op jit(solution)/shard_map/while/body/eval_jaxpr/convert_element_type | solution.py:73
  310.4 13.2 %fusion.127 = f32[12,512,1024]{2,1,0:T(8,128)} fusion(bf16[1024,12,64]{0,2,1:T(8,128)(2,1)S(1)} %get-tuple-element.505, bf16[1024,12,64]{0,2,1:T(8,128)(2,1)} %copy-done.2, s32[]{:T(128)S(6)} %select_n.59), kind=kOutput, calls=%fused_computation.33.clone.1 | convolution fusion | flops 805306368 | bytes 27525124 | tf_op jit(solution)/shard_map/while/body/eval_jaxpr/qhd,khd->hqk/dot_general | solution.py:66
  323.6 13.9 %bitcast_add_fusion.5 = f32[1024,12,64]{0,2,1:T(8,128)} fusion(f32[1024,12,64]{0,2,1:T(8,128)} %get-tuple-element.486, f32[12,512,1024]{2,1,0:T(8,128)} %fusion.127, f32[12,512]{1,0:T(8,128)S(1)} %dynamic-slice_bitcast_fusion.2, pred[512,1024]{1,0:T(8,128)(4,1)S(1)} %fusion.128, pred[]{:T(512)S(6)} %compare.3, ...), kind=kOutput, calls=%fused_computation.24.clone.1 | convolution fusion | flops 832045056 | bytes 32800772 | tf_op jit(solution)/shard_map/while/body/eval_jaxpr/hqk,qhd->khd/dot_general | solution.py:82
  337.5 18.3 %multiply_reduce_fusion.5 = (f32[12,512]{1,0:T(8,128)S(1)}, f32[12,512,1024]{2,1,0:T(8,128)}) fusion(f32[12,512,1024]{2,1,0:T(8,128)} %fusion.127, f32[12,512]{1,0:T(8,128)S(1)} %dynamic-slice_bitcast_fusion.2, pred[512,1024]{1,0:T(8,128)(4,1)S(1)} %fusion.128, bf16[1024,12,64]{0,2,1:T(8,128)(2,1)} %get-tuple-element.508, ...), kind=kOutput, calls=%fused_computation.19.clone.1 | convolution fusion | flops 836757504 | bytes 53264388 | tf_op jit(solution)/shard_map/while/body/eval_jaxpr/qhd,khd->hqk/dot_general | solution.py:69
  355.8 21.1 %multiply_convert_fusion.6 = bf16[12,512,1024]{2,1,0:T(8,128)(2,1)} fusion(f32[12,512,1024]{2,1,0:T(8,128)} %get-tuple-element.435, f32[12,512,1024]{2,1,0:T(8,128)} %fusion.127, f32[12,512]{1,0:T(8,128)S(1)} %get-tuple-element.436, f32[12,512]{1,0:T(8,128)S(1)} %dynamic-slice_bitcast_fusion.2, pred[512,1024]{1,0:T(8,128)(4,1)S(1)} %fusion.128), kind=kLoop, calls=%fused_computation.18.clone.1 | loop fusion | flops 37748736 | bytes 63488000 | tf_op jit(solution)/shard_map/while/body/eval_jaxpr/convert_element_type | solution.py:73
  411.7 13.2 %convolution_convert_fusion = bf16[3072,768]{1,0:T(8,128)(2,1)} fusion(bf16[1024,768]{0,1:T(8,128)(2,1)S(1)} %copy-done.13, f32[1024]{0:T(1024)S(1)} %copy-done.41, f32[1024,3072]{1,0:T(8,128)} %fusion.62, f32[3072]{0:T(1024)S(1)} %bitcast.109), kind=kOutput, calls=%fused_computation.54 | convolution fusion | flops 4868014080 | bytes 18890752 | tf_op jit(solution)/shard_map/tf,td->fd/dot_general | solution.py:165
  456.2 24.2 %all-reduce.15 = (bf16[768]{0:T(1024)(128)(2,1)S(1)}, bf16[768]{0:T(1024)(128)(2,1)S(1)}, bf16[768]{0:T(1024)(128)(2,1)S(1)}, bf16[1536]{0:T(1024)(128)(2,1)S(1)...) all-reduce(bf16[768]{0:T(1024)(128)(2,1)S(1)} %dynamic-update-slice, ...), channel_id=1, replica_groups=mesh['shard'=8,'rep'=4] {'shard'}, use_global_device_ids=true, to_apply=%add.6 | all-reduce | flops 9984 | bytes 39936
  480.4 36.3 %reduce-scatter.11.cloned.1.call-done = bf16[384,768]{1,0:T(8,128)(2,1)} async-done(((bf16[3072,768]{1,0:T(8,128)(2,1)}), bf16[384,768]{1,0:T(8,128)(2,1)}) %reduce-scatter.11.cloned.1.call-update) | async-done | bytes 589840 | tf_op jit(solution)/shard_map/reduce_scatter | solution.py:243
  516.8 57.3 %reduce-scatter.9.cloned.1.call-done = bf16[96,3072]{1,0:T(8,128)(2,1)} async-done(((bf16[768,3072]{1,0:T(8,128)(2,1)}), bf16[96,3072]{1,0:T(8,128)(2,1)}) %reduce-scatter.9.cloned.1.call-update) | async-done | bytes 589840 | tf_op jit(solution)/shard_map/reduce_scatter | solution.py:237
  574.1 12.2 %multiply_convert_fusion.2 = bf16[1024,768]{0,1:T(8,128)(2,1)} fusion(f32[1024,768]{0,1:T(8,128)} %copy-done.7, bf16[3072,768]{1,0:T(8,128)(2,1)} %all-gather.12.cloned.1.call-done, f32[768]{0:T(1024)S(1)} %convert_element_type.188, f32[1024]{0:T(1024)S(1)} %copy-done.41, f32[1024,3072]{1,0:T(8,128)} %fusion.62, f32[3072]{0:T(1024)S(1)} %bitcast.110), kind=kOutput, calls=%fused_computation.81 | convolution fusion | flops 4866441216 | bytes 22039552 | tf_op jit(solution)/shard_map/dot_general | solution.py:21
  587.0 12.9 %all-reduce.17 = (bf16[96]{0:T(256)(128)(2,1)S(1)}, bf16[96]{0:T(256)(128)(2,1)S(1)}, bf16[192]{0:T(256)(128)(2,1)S(1)}, bf16[96]{0:T(256)(128)(2,1)S(1)}, bf16[...) all-reduce(bf16[96]{0:T(256)(128)(2,1)S(1)} %dynamic-slice.8, ...), channel_id=1, replica_groups=mesh['shard'=8,'rep'=4] {'rep'}, use_global_device_ids=true, to_apply=%region_17.18 | all-reduce | flops 1152 | bytes 4608 | tf_op jit(solution)/shard_map/psum | solution.py:251
  614.8 39.3 %all-reduce.21.cloned.1.call-done = (bf16[96,2304]{1,0:T(8,128)(2,1)}, bf16[96,768]{1,0:T(8,128)(2,1)}, bf16[96,3072]{1,0:T(8,128)(2,1)}, bf16[384,768]{1,0:T(8,128)(2,1)}) async-done(((bf16[96,2304]{1,0:T(8,128)(2,1)}, bf16[96,768]{1,0:T(8,128)(2,1)}, bf16[96,3072]{1,0:T(8,128)(2,1)}, bf16[384,768]{1,0:T(8,128)(2,1)}), (bf16[96,2304]{1,0:T(8,128)(2,1)}, bf16[96,768]{1,0:T(8,128)(2,1)}, ...) | async-done | bytes 1769488 | tf_op jit(solution)/shard_map/psum | solution.py:253
  (270 shorter events, 210.5 us)
Async XLA Ops:
  7.2 53.2 %all-gather.6.cloned.1.call-start = ((), (), s32[]{:S(2)}) async-start(), calls=%async_computation.4 | async-start | bytes 3981312 | tf_op jit(solution)/shard_map/all_gather | solution.py:115
  7.9 148.8 %all-gather.8.cloned.1.call-start = ((), (), s32[]{:S(2)}) async-start(), calls=%async_computation.5 | async-start | bytes 1327104 | tf_op jit(solution)/shard_map/all_gather | solution.py:117
  8.7 154.1 %all-gather.10.cloned.1.call-start = ((), (), s32[]{:S(2)}) async-start(), calls=%async_computation.6 | async-start | bytes 5308416 | tf_op jit(solution)/shard_map/all_gather | solution.py:121
  9.4 164.5 %all-gather.12.cloned.1.call-start = ((), (), s32[]{:S(2)}) async-start(), calls=%async_computation.7 | async-start | bytes 5308416 | tf_op jit(solution)/shard_map/all_gather | solution.py:123
  10.0 470.4 %reduce-scatter.7.cloned.1.call-start = ((), (), s32[]{:S(2)}) async-start(), calls=%async_computation.9 | async-start | bytes 1327104 | tf_op jit(solution)/shard_map/reduce_scatter | solution.py:225
  45.7 14.7 %copy-start.34 = (f32[768]{0:T(1024)}, f32[768]{0:T(1024)S(1)}, u32[]{:S(2)}) copy-start(f32[768]{0:T(1024)S(1)} %convert_element_type.177) | copy-start | bytes 9220
  46.3 14.1 %copy-start.50 = (f32[768]{0:T(1024)}, f32[768]{0:T(1024)S(1)}, u32[]{:S(2)}) copy-start(f32[768]{0:T(1024)S(1)} %convert_element_type.178) | copy-start | bytes 9220
  76.3 24.3 %copy-start.4 = (bf16[1024,12,64]{0,2,1:T(8,128)(2,1)S(1)}, bf16[1024,12,64]{0,2,1:T(8,128)(2,1)}, u32[]{:S(2)}) copy-start(bf16[1024,12,64]{0,2,1:T(8,128)(2,1)} %get-tuple-element.466) | copy-start | bytes 4718596 | tf_op jit(solution)/shard_map/while
  87.4 16.2 %copy-start = (f32[12,512,1024]{2,1,0:T(8,128)S(1)}, f32[12,512,1024]{2,1,0:T(8,128)}, u32[]{:S(2)}) copy-start(f32[12,512,1024]{2,1,0:T(8,128)} %get-tuple-element.422) | copy-start | bytes 75497472 | tf_op jit(solution)/shard_map/while
  116.0 23.5 %copy-start.4 = (bf16[1024,12,64]{0,2,1:T(8,128)(2,1)S(1)}, bf16[1024,12,64]{0,2,1:T(8,128)(2,1)}, u32[]{:S(2)}) copy-start(bf16[1024,12,64]{0,2,1:T(8,128)(2,1)} %get-tuple-element.466) | copy-start | bytes 4718596 | tf_op jit(solution)/shard_map/while
  127.2 16.2 %copy-start = (f32[12,512,1024]{2,1,0:T(8,128)S(1)}, f32[12,512,1024]{2,1,0:T(8,128)}, u32[]{:S(2)}) copy-start(f32[12,512,1024]{2,1,0:T(8,128)} %get-tuple-element.422) | copy-start | bytes 75497472 | tf_op jit(solution)/shard_map/while
  160.7 46.4 %copy-start.24 = (f32[1024]{0:T(1024)}, f32[1024]{0:T(1024)S(1)}, u32[]{:S(2)}) copy-start(f32[1024]{0:T(1024)S(1)} %broadcast_multiply_fusion) | copy-start | bytes 12292
  162.8 44.3 %copy-start.28 = (f32[1024]{0:T(1024)}, f32[1024]{0:T(1024)S(1)}, u32[]{:S(2)}) copy-start(f32[1024]{0:T(1024)S(1)} %fusion.57) | copy-start | bytes 12292
  162.8 11.1 %copy-start.40 = (f32[1024]{0:T(1024)S(1)}, f32[1024]{0:T(1024)}, u32[]{:S(2)}) copy-start(f32[1024]{0:T(1024)} %compare_convert_fusion) | copy-start | bytes 12292
  162.8 11.1 %copy-start.44 = (f32[8,1,384]{2,1,0:T(1,128)S(1)}, f32[8,1,384]{2,1,0:T(1,128)}, u32[]{:S(2)}) copy-start(f32[8,1,384]{2,1,0:T(1,128)} %convert_element_type.217) | copy-start | bytes 36868
  173.9 17.9 %copy-start.18 = (bf16[768,3072]{1,0:T(8,128)(2,1)S(1)}, bf16[768,3072]{1,0:T(8,128)(2,1)}, u32[]{:S(2)}) copy-start(bf16[768,3072]{1,0:T(8,128)(2,1)} %all-gather.10.cloned.1.call-done) | copy-start | bytes 14155780
  213.7 266.7 %reduce-scatter.5.cloned.1.call-start = ((), (), s32[]{:S(2)}) async-start(), calls=%async_computation.8 | async-start | bytes 3981312 | tf_op jit(solution)/shard_map/reduce_scatter | solution.py:219
  222.2 13.5 %copy-start.14 = (bf16[1024,12,64]{0,2,1:T(8,128)(2,1)S(1)}, bf16[1024,12,64]{0,2,1:T(8,128)(2,1)}, u32[]{:S(2)}) copy-start(bf16[1024,12,64]{0,2,1:T(8,128)(2,1)} %get-tuple-element.507) | copy-start | bytes 4718596 | tf_op jit(solution)/shard_map/while
  310.4 13.2 %copy-start.14 = (bf16[1024,12,64]{0,2,1:T(8,128)(2,1)S(1)}, bf16[1024,12,64]{0,2,1:T(8,128)(2,1)}, u32[]{:S(2)}) copy-start(bf16[1024,12,64]{0,2,1:T(8,128)(2,1)} %get-tuple-element.507) | copy-start | bytes 4718596 | tf_op jit(solution)/shard_map/while
  377.0 9.5 %copy-start.3 = (bf16[1024,12,64]{0,2,1:T(8,128)(2,1)S(1)}, bf16[1024,12,64]{0,2,1:T(8,128)(2,1)}, u32[]{:S(2)}) copy-start(bf16[1024,12,64]{0,2,1:T(8,128)(2,1)} %copy-done.2) | copy-start | bytes 4718596 | tf_op jit(solution)/shard_map/while
  410.3 106.4 %reduce-scatter.11.cloned.1.call-start = ((), (), s32[]{:S(2)}) async-start(), calls=%async_computation.11 | async-start | bytes 5308416 | tf_op jit(solution)/shard_map/reduce_scatter | solution.py:243
  425.0 149.1 %reduce-scatter.9.cloned.1.call-start = ((), (), s32[]{:S(2)}) async-start(), calls=%async_computation.10 | async-start | bytes 5308416 | tf_op jit(solution)/shard_map/reduce_scatter | solution.py:237
  435.9 218.2 %all-reduce.21.cloned.1.call-start = ((), (), s32[]{:S(2)}) async-start(), calls=%async_computation.12 | async-start | bytes 3538944 | tf_op jit(solution)/shard_map/psum | solution.py:253
  586.4 20.3 %copy-start.43 = (f32[1024]{0:T(1024)S(1)}, f32[1024]{0:T(1024)}, u32[]{:S(2)}) copy-start(f32[1024]{0:T(1024)} %copy-done.42) | copy-start | bytes 12292
  (46 other events, 143.6 us)
Sparse Core Ops, SparseCore 0:
  9.9 36.8 all-gather.5
  48.7 24.0 all-gather.7
  74.7 38.9 all-gather.9
  115.5 38.9 all-gather.11
  213.8 37.1 reduce-scatter.6
  410.5 48.4 reduce-scatter.4
  462.8 53.8 reduce-scatter.10
  520.2 53.8 reduce-scatter.8
  576.9 77.1 all-reduce.20
where the time goes:
time: 678 us; the launch traced here: 668 us
  matrix products  271 us (40%)
  waiting for transfers between devices  136 us (20%)
  other arithmetic  109 us (16%)
  blocking collectives  71 us (10%)
  local copies, waits for them, and re-layouts  54.5 us (8%)
  between operations  18 us (3%)
  loops' own time  8.53 us (1%)
    reduce_scatter x1, waiting for transfers between devices, shards(): lax.psum_scatter(grad_expand_weight.astype(jnp.bfloat16), 'shard', scatte...  57.3 us
    unnamed x2, blocking collectives  50.2 us
    dot_general x4, matrix products, one_block(): jnp.einsum('qhd,khd->hqk', query_part, keys, preferred_element_type=jnp.f...  49.1 us
    convert_element_type x2, other arithmetic, one_block(): score_grad = (probs * (prob_grad - inner)).astype(jnp.bfloat16)  42.3 us
    psum x1, waiting for transfers between devices, shards(): lax.psum(owned[2].astype(jnp.bfloat16), 'rep').astype(jnp.float32)  39.3 us
    dot_general x2, matrix products, one_block(): jnp.einsum('qhd,khd->hqk', grad_part, values, preferred_element_type=jnp....  36.7 us
    reduce_scatter x1, waiting for transfers between devices, shards(): lax.psum_scatter(grad_reduce_weight.astype(jnp.bfloat16), 'shard', scatte...  36.3 us
    dot_general x4, matrix products, dot_float(): return jnp.dot(left, right, preferred_element_type=jnp.float32)  33.5 us
  transfers between devices with their start and end apart: 9, of which 3 were waited for; matrix products, arithmetic and copies ran while one was open for 56% of the time, Pallas kernels for 0%

commit v1 on v0

v1 whole, which is shorter than its diff:
```python
import functools

import jax
import jax.numpy as jnp
from jax import lax
from jax.experimental import pallas as pl
from jax.experimental.pallas import tpu as pltpu
from jax.sharding import PartitionSpec as P

HEAD_DIM = 64
PARTS = 8
CHUNKS = 3
EPSILON = 1e-05
BF = jnp.bfloat16
F32 = jnp.float32
NEVER = -1e30
ROOT = 0.7978845608028654
MIB = 1 << 20


def dot_nn(left, right):
    return lax.dot_general(left, right, (((1,), (0,)), ((), ())), preferred_element_type=F32)


def dot_nt(left, right):
    return lax.dot_general(left, right, (((1,), (1,)), ((), ())), preferred_element_type=F32)


def dot_tn(left, right):
    return lax.dot_general(left, right, (((0,), (0,)), ((), ())), preferred_element_type=F32)


def normalise(values):
    center = values - jnp.mean(values, axis=-1, keepdims=True)
    variance = jnp.mean(center * center, axis=-1, keepdims=True)
    scale = lax.rsqrt(variance + EPSILON)
    return center * scale, scale


def norm_back(values, incoming, gain):
    unit, scale = normalise(values)
    scaled = incoming * gain
    first = jnp.mean(scaled, axis=-1, keepdims=True)
    second = jnp.mean(scaled * unit, axis=-1, keepdims=True)
    back = scale * (scaled - first - unit * second)
    return back, jnp.sum(incoming * unit, axis=0, keepdims=True)


def whole_spec(shape):
    return pl.BlockSpec(shape, lambda *_: (0,) * len(shape))


def params(mib):
    return pltpu.CompilerParams(vmem_limit_bytes=mib * MIB)


def cost(flops, moved, exps=0):
    return pl.CostEstimate(flops=int(flops), bytes_accessed=int(moved), transcendentals=int(exps))


def fill_weight(order_ref, pack_ref, first, blocks, out_ref, rows, lead=None):
    mine = order_ref[0]
    for part in range(PARTS):
        piece = part ^ mine
        for at in range(blocks):
            tile = pack_ref[piece, first + at * rows : first + (at + 1) * rows, :]
            if lead is None:
                out_ref[part * rows : (part + 1) * rows, at * 128 : (at + 1) * 128] = tile
            else:
                group, inside = divmod(at, lead)
                out_ref[group, part * rows : (part + 1) * rows, inside * 128 : (inside + 1) * 128] = tile


def project_kernel(width, order_ref, pack_ref, x_ref, gain_ref, shift_ref, bias_ref, qkv_ref, turned_ref, w_ref):
    @pl.when(pl.program_id(0) == 0)
    def _():
        fill_weight(order_ref, pack_ref, 0, 3 * width // 128, w_ref, width // PARTS, width // 128)

    unit, _ = normalise(x_ref[...].astype(F32))
    normed = (unit * gain_ref[...] + shift_ref[...]).astype(BF)
    turned_ref[...] = normed.T
    for at in range(3):
        qkv_ref[at] = (dot_nn(normed, w_ref[at]) + bias_ref[at]).astype(BF)


def project(order, pack, x, gain, shift, bias):
    rows, width = x.shape
    block = min(256, rows)
    return pl.pallas_call(
        functools.partial(project_kernel, width),
        grid_spec=pltpu.PrefetchScalarGridSpec(
            num_scalar_prefetch=1,
            grid=(rows // block,),
            in_specs=[
                whole_spec(pack.shape),
                pl.BlockSpec((block, width), lambda i, *_: (i, 0)),
                whole_spec(gain.shape),
                whole_spec(shift.shape),
                whole_spec(bias.shape),
            ],
            out_specs=[
                pl.BlockSpec((3, block, width), lambda i, *_: (0, i, 0)),
                pl.BlockSpec((width, block), lambda i, *_: (0, i)),
            ],
            scratch_shapes=[pltpu.VMEM((3, width, width), BF)],
        ),
        out_shape=[
            jax.ShapeDtypeStruct((3, rows, width), BF),
            jax.ShapeDtypeStruct((width, rows), BF),
        ],
        compiler_params=params(40),
        cost_estimate=cost(6 * rows * width * width, 14 * rows * width),
        name="project",
    )(order, pack, x, gain, shift, bias)


def attend_forward_kernel(block, col_ref, row_ref, qkv_ref, mixed_ref, log_ref, bias_ref):
    rows = row_ref.shape[1]

    @pl.when(pl.program_id(0) == 0)
    def _():
        for first in range(0, rows, block):
            at = lax.broadcasted_iota(jnp.int32, (block, rows), 0) + first
            key = lax.broadcasted_iota(jnp.int32, (block, rows), 1)
            same = col_ref[first : first + block, :] == row_ref[...]
            bias_ref[first : first + block, :] = jnp.where(same & (key <= at), 0.0, NEVER)

    lane = lax.broadcasted_iota(jnp.int32, (block, 128), 1)
    for first in range(0, rows, block):
        last = first + block
        queries = qkv_ref[0, first:last, :] * jnp.asarray(0.125, BF)
        outs, logs = [], []
        for head in range(2):
            mine = (lane < HEAD_DIM) if head == 0 else (lane >= HEAD_DIM)
            scores = dot_nt(jnp.where(mine, queries, jnp.zeros_like(queries)), qkv_ref[1, :last, :])
            scores = scores + bias_ref[first:last, :last]
            largest = jnp.max(scores, axis=-1, keepdims=True)
            expo = jnp.exp(scores - largest)
            total = jnp.sum(expo, axis=-1, keepdims=True)
            outs.append(dot_nn(expo.astype(BF), qkv_ref[2, :last, :]) / total)
            logs.append(largest + jnp.log(total))
        mixed_ref[first:last, :] = jnp.where(lane < HEAD_DIM, outs[0], outs[1]).astype(BF)
        log_ref[0, first:last, :] = jnp.where(lane < HEAD_DIM, logs[1], logs[0])


def attend_forward(col, row, qkv):
    _, rows, width = qkv.shape
    pairs = width // 128
    block = min(256, rows)
    return pl.pallas_call(
        functools.partial(attend_forward_kernel, block),
        grid=(pairs,),
        in_specs=[
            whole_spec(col.shape),
            whole_spec(row.shape),
            pl.BlockSpec((3, rows, 128), lambda i: (0, 0, i)),
        ],
        out_specs=[
            pl.BlockSpec((rows, 128), lambda i: (0, i)),
            pl.BlockSpec((1, rows, 128), lambda i: (i, 0, 0)),
        ],
        scratch_shapes=[pltpu.VMEM((rows, rows), F32)],
        out_shape=[
            jax.ShapeDtypeStruct((rows, width), BF),
            jax.ShapeDtypeStruct((pairs, rows, 128), F32),
        ],
        compiler_params=params(32),
        cost_estimate=cost(16 * rows * rows * width, 12 * rows * width, rows * rows * pairs),
        name="attend_forward",
    )(col, row, qkv)


def split_lanes(value, lane):
    high = value.astype(BF)
    rest = value - high.astype(F32)
    middle = rest.astype(BF)
    low = (rest - middle.astype(F32)).astype(BF)
    inside = lax.rem(lane, HEAD_DIM)
    zero = jnp.zeros_like(high)
    return jnp.where(inside == 0, high, jnp.where(inside == 1, middle, jnp.where(inside == 2, low, zero)))


def attend_backward_kernel(
    block, col_ref, row_ref, qkv_ref, mixed_ref, log_ref, grad_ref, out_ref, bias_ref, q_ref, k_ref, d_ref, v_ref, dq_ref
):
    rows = row_ref.shape[1]

    @pl.when(pl.program_id(0) == 0)
    def _():
        for first in range(0, rows, block):
            key = lax.broadcasted_iota(jnp.int32, (block, rows), 0) + first
            at = lax.broadcasted_iota(jnp.int32, (block, rows), 1)
            same = col_ref[first : first + block, :] == row_ref[...]
            bias_ref[first : first + block, :] = jnp.where(same & (key <= at), 0.0, NEVER)

    lane = lax.broadcasted_iota(jnp.int32, (block, 128), 1)
    below = lane < HEAD_DIM
    minus = jnp.where(lax.rem(lane, HEAD_DIM) < 3, -1.0, 0.0).astype(BF)
    for first in range(0, rows, block):
        last = first + block
        queries = qkv_ref[0, first:last, :] * jnp.asarray(0.125, BF)
        keys = qkv_ref[1, first:last, :]
        values = qkv_ref[2, first:last, :]
        grads = grad_ref[first:last, :]
        product = grads.astype(F32) * mixed_ref[first:last, :].astype(F32)
        sums = [
            jnp.sum(jnp.where(below, product, 0.0), axis=-1, keepdims=True),
            jnp.sum(jnp.where(below, 0.0, product), axis=-1, keepdims=True),
        ]
        logs = split_lanes(log_ref[0, first:last, :], lane)
        inner = split_lanes(jnp.where(below, sums[1], sums[0]), lane)
        for head in range(2):
            mine = below if head == 0 else lane >= HEAD_DIM
            q_ref[head, first:last, :] = jnp.where(mine, queries, logs)
            k_ref[head, first:last, :] = jnp.where(mine, keys, minus)
            d_ref[head, first:last, :] = jnp.where(mine, grads, inner)
            v_ref[head, first:last, :] = jnp.where(mine, values, minus)

    for first in range(0, rows, block):
        last = first + block
        key_parts, value_parts, query_parts = [], [], []
        for head in range(2):
            scores = dot_nt(k_ref[head, first:last, :], q_ref[head, first:, :]) + bias_ref[first:last, first:]
            probs = jnp.exp(scores)
            slopes = probs * dot_nt(v_ref[head, first:last, :], d_ref[head, first:, :])
            slopes = slopes.astype(BF)
            value_parts.append(dot_nn(probs.astype(BF), d_ref[head, first:, :]))
            key_parts.append(dot_nn(slopes, q_ref[head, first:, :]))
            query_parts.append(dot_tn(slopes, k_ref[head, first:last, :]))
        out_ref[1, first:last, :] = jnp.where(below, key_parts[0], key_parts[1]).astype(BF)
        out_ref[2, first:last, :] = jnp.where(below, value_parts[0], value_parts[1]).astype(BF)
        side = lax.broadcasted_iota(jnp.int32, (rows - first, 128), 1) < HEAD_DIM
        part = jnp.where(side, query_parts[0], query_parts[1])
        if first == 0:
            dq_ref[...] = part
        else:
            dq_ref[first:, :] += part
    out_ref[0] = (dq_ref[...] * 0.125).astype(BF)


def attend_backward(col, row, qkv, mixed, log_total, grad):
    _, rows, width = qkv.shape
    pairs = width // 128
    block = min(256, rows)
    return pl.pallas_call(
        functools.partial(attend_backward_kernel, block),
        grid=(pairs,),
        in_specs=[
            whole_spec(col.shape),
            whole_spec(row.shape),
            pl.BlockSpec((3, rows, 128), lambda i: (0, 0, i)),
            pl.BlockSpec((rows, 128), lambda i: (0, i)),
            pl.BlockSpec((1, rows, 128), lambda i: (i, 0, 0)),
            pl.BlockSpec((rows, 128), lambda i: (0, i)),
        ],
        out_specs=pl.BlockSpec((3, rows, 128), lambda i: (0, 0, i)),
        scratch_shapes=[pltpu.VMEM((rows, rows), F32)]
        + [pltpu.VMEM((2, rows, 128), BF)] * 4
        + [pltpu.VMEM((rows, 128), F32)],
        out_shape=jax.ShapeDtypeStruct((3, rows, width), BF),
        compiler_params=params(40),
        cost_estimate=cost(40 * rows * rows * width, 20 * rows * width, rows * rows * pairs),
        name="attend_backward",
    )(col, row, qkv, mixed, log_total, grad)


def middle_kernel(
    width, order_ref, pack_ref, x_ref, mixed_ref, seg_ref, cot_ref, bias_ref, gain_ref, shift_ref,
    middle_ref, normed_ref, turned_ref, feed_ref, w_ref
):
    @pl.when(pl.program_id(0) == 0)
    def _():
        fill_weight(order_ref, pack_ref, 0, width // 128, w_ref, width // PARTS)

    middle = x_ref[...].astype(F32) + dot_nn(mixed_ref[...], w_ref[...]) + bias_ref[...]
    middle_ref[...] = middle
    unit, _ = normalise(middle)
    normed = (unit * gain_ref[...] + shift_ref[...]).astype(BF)
    normed_ref[...] = normed
    turned_ref[...] = normed.T
    live = seg_ref[...] >= 0
    feed_ref[...] = jnp.where(live, cot_ref[...].astype(F32), 0.0).astype(BF)


def make_middle(order, pack, x, mixed, col, cot, bias, gain, shift):
    rows, width = x.shape
    block = min(256, rows)
    by_rows = pl.BlockSpec((block, width), lambda i, *_: (i, 0))
    return pl.pallas_call(
        functools.partial(middle_kernel, width),
        grid_spec=pltpu.PrefetchScalarGridSpec(
            num_scalar_prefetch=1,
            grid=(rows // block,),
            in_specs=[
                whole_spec(pack.shape),
                by_rows,
                by_rows,
                pl.BlockSpec((block, 1), lambda i, *_: (i, 0)),
                by_rows,
                whole_spec(bias.shape),
                whole_spec(gain.shape),
                whole_spec(shift.shape),
            ],
            out_specs=[by_rows, by_rows, pl.BlockSpec((width, block), lambda i, *_: (0, i)), by_rows],
            scratch_shapes=[pltpu.VMEM((width, width), BF)],
        ),
        out_shape=[
            jax.ShapeDtypeStruct((rows, width), F32),
            jax.ShapeDtypeStruct((rows, width), BF),
            jax.ShapeDtypeStruct((width, rows), BF),
            jax.ShapeDtypeStruct((rows, width), BF),
        ],
        compiler_params=params(32),
        cost_estimate=cost(2 * rows * width * width, 16 * rows * width),
        name="middle",
    )(order, pack, x, mixed, col, cot, bias, gain, shift)


def feed_kernel(
    width, hidden, steps, has_sum, order_ref, pack_ref, normed_ref, turned_ref, feed_ref, bias_ref, *refs
):
    if has_sum:
        out_in_ref, back_in_ref, *refs = refs
    out_ref, back_ref, grad_ref, sum_ref, we_ref, wr_ref, h_ref, e_ref = refs
    step = pl.program_id(0)
    block = normed_ref.shape[0]
    share = width // PARTS
    mine = order_ref[0]

    @pl.when(step == 0)
    def _():
        fill_weight(order_ref, pack_ref, 0, hidden // 128, we_ref, share)
        fill_weight(order_ref, pack_ref, hidden // 128 * share, width // 128, wr_ref, hidden // PARTS)

    @pl.when(step < steps)
    def _():
        here = pl.ds(pl.multiple_of(step * block, block), block)
        normed = normed_ref[...]
        feed = feed_ref[here, :]
        for at in range(0, hidden, 256):
            cols = slice(at, at + 256)
            u = dot_nn(normed, we_ref[:, cols]) + bias_ref[:, cols]
            hidden_grad = dot_nt(feed, wr_ref[cols, :])
            square = u * u
            tanh = jnp.tanh(ROOT * u * (1.0 + 0.044715 * square))
            half = 0.5 + 0.5 * tanh
            h_ref[here, cols] = (u * half).astype(BF)
            slope = half + (0.5 * ROOT) * u * (1.0 - tanh * tanh) * (1.0 + (3 * 0.044715) * square)
            e_ref[here, cols] = (hidden_grad * slope).astype(BF)
        out = dot_nn(h_ref[here, :], wr_ref[...])
        back = dot_nt(e_ref[here, :], we_ref[...])
        if has_sum:
            out = out + out_in_ref[...]
            back = back + back_in_ref[...]
        out_ref[...] = out
        back_ref[...] = back

    @pl.when(step >= steps)
    def _():
        at = step - steps
        cols = pl.ds(pl.multiple_of(at * 256, 256), 256)
        e_part = e_ref[:, cols]
        sum_ref[:, cols] = jnp.sum(e_part.astype(F32), axis=0, keepdims=True)
        grad = dot_nn(turned_ref[...], e_part).astype(BF)
        for side in range(2):
            base = pl.multiple_of((2 * at + side) * share, share)
            for part in range(PARTS):
                grad_ref[part ^ mine, pl.ds(base, share), :] = grad[
                    part * share : (part + 1) * share, side * 128 : (side + 1) * 128
                ]
        grad = dot_tn(h_ref[:, cols], feed_ref[...]).astype(BF)
        first = hidden // 128 * share
        for side in range(2):
            part = (2 * at + side) ^ mine
            for lane in range(width // 128):
                grad_ref[part, first + lane * 128 : first + (lane + 1) * 128, :] = grad[
                    side * 128 : (side + 1) * 128, lane * 128 : (lane + 1) * 128
                ]


def feed_chunk(order, pack, normed, turned, feed, bias, sums):
    rows, width = normed.shape
    hidden = bias.shape[1]
    block = min(256, rows)
    steps = rows // block
    by_rows = pl.BlockSpec((block, width), lambda i, *_: (jnp.minimum(i, steps - 1), 0))
    return pl.pallas_call(
        functools.partial(feed_kernel, width, hidden, steps, bool(sums)),
        grid_spec=pltpu.PrefetchScalarGridSpec(
            num_scalar_prefetch=1,
            grid=(steps + hidden // 256,),
            in_specs=[
                whole_spec(pack.shape),
                by_rows,
                whole_spec(turned.shape),
                whole_spec(feed.shape),
                whole_spec(bias.shape),
            ]
            + [by_rows] * len(sums),
            out_specs=[by_rows, by_rows, whole_spec(pack.shape), whole_spec((1, hidden))],
            scratch_shapes=[
                pltpu.VMEM((width, hidden), BF),
                pltpu.VMEM((hidden, width), BF),
                pltpu.VMEM((rows, hidden), BF),
                pltpu.VMEM((rows, hidden), BF),
            ],
        ),
        out_shape=[
            jax.ShapeDtypeStruct((rows, width), F32),
            jax.ShapeDtypeStruct((rows, width), F32),
            jax.ShapeDtypeStruct(pack.shape, BF),
            jax.ShapeDtypeStruct((1, hidden), F32),
        ],
        compiler_params=params(48),
        cost_estimate=cost(12 * rows * width * hidden, 20 * rows * width, rows * hidden),
        name="feed",
    )(order, pack, normed, turned, feed, bias, *sums)


def branch_kernel(
    width, steps, order_ref, pack_ref, back_ref, middle_ref, sum_ref, feed_ref, seg_ref, mixed_ref, gain_ref, bias_ref,
    out_ref, grad_ref, mixed_grad_ref, pack_grad_ref, sums_ref, w_ref, b_ref, t_ref
):
    step = pl.program_id(0)
    block = back_ref.shape[0]
    share = width // PARTS
    mine = order_ref[0]

    @pl.when(step == 0)
    def _():
        fill_weight(order_ref, pack_ref, 0, width // 128, w_ref, share)
        sums_ref[...] = jnp.zeros_like(sums_ref)

    middle = middle_ref[...]
    live = seg_ref[...] >= 0
    out_ref[...] = jnp.where(live, middle + sum_ref[...] + bias_ref[...], 0.0).astype(BF)
    back = back_ref[...]
    feed = feed_ref[...].astype(F32)
    part, gain_sum = norm_back(middle, back, gain_ref[...])
    grad = feed + part
    grad_ref[...] = grad
    branch = grad.astype(BF)
    b_ref[pl.ds(pl.multiple_of(step * block, block), block), :] = branch
    mixed_grad_ref[...] = dot_nt(branch, w_ref[...]).astype(BF)
    sums_ref[0:1, :] += gain_sum
    sums_ref[1:2, :] += jnp.sum(back, axis=0, keepdims=True)
    sums_ref[2:3, :] += jnp.sum(branch.astype(F32), axis=0, keepdims=True)
    sums_ref[3:4, :] += jnp.sum(feed, axis=0, keepdims=True)

    @pl.when(step == steps - 1)
    def _():
        for first in range(0, width, 256):
            t_ref[first : first + 256, :] = dot_tn(mixed_ref[:, first : first + 256], b_ref[...]).astype(BF)
        for part in range(PARTS):
            for lane in range(width // 128):
                pack_grad_ref[part ^ mine, lane * share : (lane + 1) * share, :] = t_ref[
                    part * share : (part + 1) * share, lane * 128 : (lane + 1) * 128
                ]


def branch(order, pack, back, middle, total, feed, col, mixed, gain, bias):
    rows, width = middle.shape
    block = min(256, rows)
    steps = rows // block
    by_rows = pl.BlockSpec((block, width), lambda i, *_: (i, 0))
    return pl.pallas_call(
        functools.partial(branch_kernel, width, steps),
        grid_spec=pltpu.PrefetchScalarGridSpec(
            num_scalar_prefetch=1,
            grid=(steps,),
            in_specs=[
                whole_spec(pack.shape),
                by_rows,
                by_rows,
                by_rows,
                by_rows,
                pl.BlockSpec((block, 1), lambda i, *_: (i, 0)),
                whole_spec(mixed.shape),
                whole_spec(gain.shape),
                whole_spec(bias.shape),
            ],
            out_specs=[by_rows, by_rows, by_rows, whole_spec(pack.shape), whole_spec((8, width))],
            scratch_shapes=[
                pltpu.VMEM((width, width), BF),
                pltpu.VMEM((rows, width), BF),
                pltpu.VMEM((width, width), BF),
            ],
        ),
        out_shape=[
            jax.ShapeDtypeStruct((rows, width), BF),
            jax.ShapeDtypeStruct((rows, width), F32),
            jax.ShapeDtypeStruct((rows, width), BF),
            jax.ShapeDtypeStruct(pack.shape, BF),
            jax.ShapeDtypeStruct((8, width), F32),
        ],
        compiler_params=params(40),
        cost_estimate=cost(4 * rows * width * width, 24 * rows * width),
        name="branch",
    )(order, pack, back, middle, total, feed, col, mixed, gain, bias)


def triple_kernel(width, order_ref, turned_ref, grad_ref, pack_ref, sum_ref):
    share = width // PARTS
    mine = order_ref[0]
    grads = grad_ref[0]
    sum_ref[...] = jnp.sum(grads.astype(F32), axis=0, keepdims=True)
    product = dot_nn(turned_ref[...], grads).astype(BF)
    for side in range(2):
        for part in range(PARTS):
            pack_ref[part ^ mine, side * share : (side + 1) * share, :] = product[
                part * share : (part + 1) * share, side * 128 : (side + 1) * 128
            ]


def triple_grad(order, turned, grads):
    width, rows = turned.shape
    share = width // PARTS
    per = width // 256
    return pl.pallas_call(
        functools.partial(triple_kernel, width),
        grid_spec=pltpu.PrefetchScalarGridSpec(
            num_scalar_prefetch=1,
            grid=(3 * per,),
            in_specs=[
                whole_spec(turned.shape),
                pl.BlockSpec((1, rows, 256), lambda i, *_: (i // per, 0, i % per)),
            ],
            out_specs=[
                pl.BlockSpec((PARTS, 2 * share, 128), lambda i, *_: (0, i, 0)),
                pl.BlockSpec((1, 256), lambda i, *_: (0, i)),
            ],
        ),
        out_shape=[
            jax.ShapeDtypeStruct((PARTS, 3 * width // 128 * share, 128), BF),
            jax.ShapeDtypeStruct((1, 3 * width), F32),
        ],
        compiler_params=params(32),
        cost_estimate=cost(6 * rows * width * width, 12 * rows * width),
        name="triple_grad",
    )(order, turned, grads)


def input_kernel(width, order_ref, pack_ref, x_ref, grads_ref, middle_ref, gain_ref, out_ref, sums_ref, w_ref):
    @pl.when(pl.program_id(0) == 0)
    def _():
        fill_weight(order_ref, pack_ref, 0, 3 * width // 128, w_ref, width // PARTS, width // 128)
        sums_ref[...] = jnp.zeros_like(sums_ref)

    back = dot_nt(grads_ref[0], w_ref[0]) + dot_nt(grads_ref[1], w_ref[1]) + dot_nt(grads_ref[2], w_ref[2])
    part, gain_sum = norm_back(x_ref[...].astype(F32), back, gain_ref[...])
    out_ref[...] = (middle_ref[...] + part).astype(BF)
    sums_ref[0:1, :] += gain_sum
    sums_ref[1:2, :] += jnp.sum(back, axis=0, keepdims=True)


def input_grad(order, pack, x, grads, middle_grad, gain):
    rows, width = x.shape
    block = min(256, rows)
    by_rows = pl.BlockSpec((block, width), lambda i, *_: (i, 0))
    return pl.pallas_call(
        functools.partial(input_kernel, width),
        grid_spec=pltpu.PrefetchScalarGridSpec(
            num_scalar_prefetch=1,
            grid=(rows // block,),
            in_specs=[
                whole_spec(pack.shape),
                by_rows,
                pl.BlockSpec((3, block, width), lambda i, *_: (0, i, 0)),
                by_rows,
                whole_spec(gain.shape),
            ],
            out_specs=[by_rows, whole_spec((8, width))],
            scratch_shapes=[pltpu.VMEM((3, width, width), BF)],
        ),
        out_shape=[
            jax.ShapeDtypeStruct((rows, width), BF),
            jax.ShapeDtypeStruct((8, width), F32),
        ],
        compiler_params=params(40),
        cost_estimate=cost(6 * rows * width * width, 18 * rows * width),
        name="input_grad",
    )(order, pack, x, grads, middle_grad, gain)


def tiles(matrix):
    rows, cols = matrix.shape
    return matrix.reshape(rows, cols // 128, 128).transpose(1, 0, 2).reshape(-1, 128)


def untiles(packed, rows):
    return packed.reshape(-1, rows, 128).transpose(1, 0, 2).reshape(rows, -1)


def scatter(part):
    return lax.psum(lax.psum_scatter(part, "shard", scatter_dimension=0, tiled=True), "rep")


def pack_weights(triple, output, expand, reduce, vectors):
    share, width = output.shape
    flat = jnp.concatenate(vectors)
    flat = jnp.pad(flat, (0, 2048 - flat.shape[0])).reshape(16, 128)
    up = expand.reshape(share, PARTS, CHUNKS, 128)
    down = reduce.reshape(CHUNKS, 128, width)
    return (
        jnp.concatenate([tiles(triple), flat]),
        tiles(output),
        *[jnp.concatenate([tiles(up[:, :, at].reshape(share, -1)), tiles(down[at])]) for at in range(CHUNKS)],
    )


def unpack_grads(share, grad_a, grad_b, *grads_c):
    half = PARTS * share
    ups = [untiles(one[:half], share).reshape(share, PARTS, 1, 128) for one in grads_c]
    downs = [untiles(one[half:], 128) for one in grads_c]
    return (
        untiles(grad_a, share),
        untiles(grad_b, share),
        jnp.concatenate(ups, axis=2).reshape(share, -1),
        jnp.concatenate(downs, axis=0),
    )


def shards(
    count,
    tokens,
    segments,
    cotangent,
    attend_gain,
    attend_shift,
    triple_weight,
    triple_bias,
    output_weight,
    output_bias,
    feed_gain,
    feed_shift,
    expand_weight,
    expand_bias,
    reduce_weight,
    reduce_bias,
):
    rows, width = tokens.shape
    small = (
        attend_gain, attend_shift, triple_bias, output_bias, feed_gain, feed_shift, expand_bias, reduce_bias
    )
    order = jnp.zeros((1,), jnp.int32)
    share = width // PARTS
    weights = (triple_weight, output_weight, expand_weight, reduce_weight, small)
    if count == PARTS:
        packs = [
            lax.all_gather(one, "shard", axis=0, tiled=True).reshape(PARTS, -1, 128) for one in pack_weights(*weights)
        ]
    else:
        weights = jax.tree.map(lambda one: lax.all_gather(one, "shard", axis=0, tiled=True), weights)
        weights = jax.tree.map(lambda one: one.reshape(PARTS, -1, *one.shape[1:]), weights)
        packs = jax.vmap(pack_weights)(*weights)
    pack_a, pack_b, *pack_c = packs
    vectors = pack_a[:, -16:, :].reshape(PARTS, 2048).astype(F32)
    whole, at = [], 0
    for one in small:
        size = one.shape[0] * count // PARTS
        whole.append(vectors[:, at : at + size].reshape(1, -1))
        at += size
    gain_one, shift_one, bias_qv, bias_out, gain_two, shift_two, bias_up, bias_down = whole
    bias_qkv = jnp.concatenate([bias_qv[:, :width], jnp.zeros((1, width), F32), bias_qv[:, width:]], axis=1)
    bias_qkv = bias_qkv.reshape(3, 1, width)
    bias_up = bias_up.reshape(PARTS, CHUNKS, 128)
    col = segments.reshape(rows, 1)
    row = segments.reshape(1, rows)

    qkv, turned_one = project(order, pack_a, tokens, gain_one, shift_one, bias_qkv)
    mixed, log_total = attend_forward(col, row, qkv)
    middle, normed_two, turned_two, feed = make_middle(
        order, pack_b, tokens, mixed, col, cotangent, bias_out, gain_two, shift_two
    )
    sums = ()
    grads_c, sums_c = [], []
    for at in range(CHUNKS):
        out_sum, back_sum, grad_c, sum_c = feed_chunk(
            order, pack_c[at], normed_two, turned_two, feed, bias_up[:, at].reshape(1, -1), sums
        )
        sums = (out_sum, back_sum)
        grads_c.append(grad_c)
        sums_c.append(sum_c.reshape(PARTS, 128))
    out_tokens, middle_grad, mixed_grad, grad_b, sums_two = branch(
        order, pack_b, back_sum, middle, out_sum, feed, col, mixed, gain_two, bias_down
    )
    projected_grad = attend_backward(col, row, qkv, mixed, log_total, mixed_grad)
    grad_a, sums_qkv = triple_grad(order, turned_one, projected_grad)
    grad_tokens, sums_one = input_grad(order, pack_a, tokens, projected_grad, middle_grad, gain_one)

    vectors = jnp.concatenate(
        [
            sums_one[0].reshape(PARTS, -1),
            sums_one[1].reshape(PARTS, -1),
            jnp.concatenate([sums_qkv[:, :width], sums_qkv[:, 2 * width :]], axis=1).reshape(PARTS, -1),
            sums_two[2].reshape(PARTS, -1),
            sums_two[0].reshape(PARTS, -1),
            sums_two[1].reshape(PARTS, -1),
            sums_c[0],
            sums_c[1],
            sums_c[2],
            sums_two[3].reshape(PARTS, -1),
        ],
        axis=1,
    )
    vectors = vectors.astype(BF)
    grads = (grad_a, grad_b, *grads_c)
    if count == PARTS:
        grads = [scatter(one.reshape(-1, 128)) for one in grads]
        grads = unpack_grads(share, *grads)
        vectors = jnp.pad(vectors, ((0, 0), (0, 2048 - vectors.shape[1]))).reshape(-1, 128)
        vectors = scatter(vectors).reshape(-1)
        small_grads, at = [], 0
        for one in small:
            small_grads.append(vectors[at : at + one.shape[0]])
            at += one.shape[0]
    else:
        grads = jax.vmap(functools.partial(unpack_grads, share))(*grads)
        grads = [scatter(one.reshape(-1, one.shape[-1])) for one in grads]
        small_grads, at = [], 0
        for one in small:
            size = one.shape[0] * count // PARTS
            small_grads.append(scatter(vectors[:, at : at + size].reshape(-1)))
            at += size
    grads = [one.astype(F32) for one in grads]
    small_grads = [one.astype(F32) for one in small_grads]
    return (
        out_tokens,
        grad_tokens,
        small_grads[0],
        small_grads[1],
        grads[0],
        small_grads[2],
        grads[1],
        small_grads[3],
        small_grads[4],
        small_grads[5],
        grads[2],
        small_grads[6],
        grads[3],
        small_grads[7],
    )


def solution(mesh):
    return jax.shard_map(
        functools.partial(shards, mesh.shape["shard"]),
        mesh=mesh,
        in_specs=(
            P(("shard", "rep"), None),
            P(("shard", "rep")),
            P(("shard", "rep"), None),
            P("shard"),
            P("shard"),
            P("shard", None),
            P("shard"),
            P("shard", None),
            P("shard"),
            P("shard"),
            P("shard"),
            P("shard", None),
            P("shard"),
            P("shard", None),
            P("shard"),
        ),
        out_specs=(
            P(("shard", "rep"), None),
            P(("shard", "rep"), None),
            P("shard"),
            P("shard"),
            P("shard", None),
            P("shard"),
            P("shard", None),
            P("shard"),
            P("shard"),
            P("shard"),
            P("shard", None),
            P("shard"),
            P("shard", None),
            P("shard"),
        ),
        check_vma=False,
    )
```

time: 678 us -> 589 us (0.87); the launches traced: 668 us -> 588 us
  matrix products: 271 us -> 0 us
  waiting for transfers between devices: 136 us -> 347 us
  Pallas kernels: 0 us -> 138 us
  other arithmetic: 109 us -> 8.78 us
  blocking collectives: 71 us -> 11.8 us
  local copies, waits for them, and re-layouts: 54.5 us -> 66.8 us
  loops' own time: 8.53 us -> 0 us
    dot_general x26 -> x0, matrix products: 271 us -> none  [the longest x4 49.1 us: one_block(): jnp.einsum('qhd,khd->hqk', query_part, keys, preferred_element_type=jnp.f...]
    pallas_call x0 -> x10, Pallas kernels: none -> 138 us  [the longest x3 53.8 us: feed_chunk(): pl.pallas_call(functools.partial(feed_kernel, width, hidden, steps, bool(...]
    reduce_scatter x4 -> x6, waiting for transfers between devices: 93.7 us -> 211 us  [scatter(): lax.psum_scatter(part, 'shard', scatter_dimension=0, tiled=True)]
    all_gather x4 -> x5, waiting for transfers between devices: 0.04 us -> 66.8 us  [shards(): lax.all_gather(one, 'shard', axis=0, tiled=True).reshape(PARTS, -1, 128)]
    convert_element_type x23 -> x7, other arithmetic: 62.7 us -> 4.77 us  [the longest x4 2.88 us: shards(): grads = [one.astype(F32) for one in grads]]
    unnamed x2 -> x0, blocking collectives: 50.2 us -> none
    reduce_sum x11 -> x0, other arithmetic: 37.9 us -> none  [the longest x2 25.4 us: one_block(): totals = jnp.sum(expo, axis=-1, keepdims=True)]
    psum x1, waiting for transfers between devices: 39.3 us -> 67 us  [scatter(): lax.psum(lax.psum_scatter(part, 'shard', scatter_dimension=0, tiled=True)...]
  transfers between devices with their start and end apart: 9 -> 12, of which waited for: 3 -> 10; matrix products, arithmetic and copies ran while one was open for 56% -> 3% of each run, Pallas kernels for 0% -> 19%
where the time goes in v1:
time: 589 us; the launch traced here: 588 us
  waiting for transfers between devices  347 us (59%)
  Pallas kernels  138 us (23%)
  local copies, waits for them, and re-layouts  66.8 us (11%)
  between operations  14.7 us (2%)
  blocking collectives  11.8 us (2%)
  other arithmetic  8.78 us (1%)
    reduce_scatter x6, waiting for transfers between devices, scatter(): lax.psum_scatter(part, 'shard', scatter_dimension=0, tiled=True)  211 us
    psum x1, waiting for transfers between devices, scatter(): lax.psum(lax.psum_scatter(part, 'shard', scatter_dimension=0, tiled=True)...  67 us
    all_gather x5, waiting for transfers between devices, shards(): lax.all_gather(one, 'shard', axis=0, tiled=True).reshape(PARTS, -1, 128)  66.8 us
    pallas_call x3, Pallas kernels, feed_chunk(): pl.pallas_call(functools.partial(feed_kernel, width, hidden, steps, bool(...  53.8 us
    unnamed x87, local copies, waits for them, and re-layouts  46.5 us
    pallas_call x1, Pallas kernels, attend_backward(): pl.pallas_call(functools.partial(attend_backward_kernel, block), grid=(pa...  29 us
    pallas_call x1, Pallas kernels, attend_forward(): pl.pallas_call(functools.partial(attend_forward_kernel, block), grid=(pai...  21.3 us
    psum x1, blocking collectives, scatter(): lax.psum(lax.psum_scatter(part, 'shard', scatter_dimension=0, tiled=True)...  11.8 us
  transfers between devices with their start and end apart: 12, of which 10 were waited for; matrix products, arithmetic and copies ran while one was open for 3% of the time, Pallas kernels for 19%

profile of v1, /device:TPU:0, one launch (start us, length us, event | category | flops | bytes accessed | tf_op | source)
XLA Modules:
  0.0 587.7 jit_solution(8396458430601196436)
XLA Ops:
  7.2 5.4 concatenate.33
  22.0 29.9 %all-gather.10.cloned.1.call-done = bf16[13952,128]{1,0:T(8,128)(2,1)} async-done(((bf16[1744,128]{1,0:T(8,128)(2,1)}), bf16[13952,128]{1,0:T(8,128)(2,1)}) %all-gather.10.cloned.1.call-update) | async-done | bytes 3571728 | tf_op jit(solution)/shard_map/all_gather | solution.py:650
  55.4 6.2 %project.1 = (bf16[3,1024,768]{2,1,0:T(8,128)(2,1)S(1)}, bf16[768,1024]{1,0:T(8,128)(2,1)S(1)}) custom-call(s32[1]{0:T(128)} %constant.1.clone.1.order_ref, bf16[8,1744,128]{2,1,0:T(8,128)(2,1)S(1)} %bitcast.117, bf16[1024,768]{1,0:T(8,128)(2,1)S(1)} %copy-done.10, f32[1,768]{1,0:T(1,128)S(1)} %reshape.211.gain_ref, f32[1,768]{1,0:T(1,128)S(1)} %reshape.212.shift_ref, ...), custom_call_target="tpu_custom_call" | custom-call | flops 3623878656 | bytes 11010048 | tf_op jit(solution)/shard_map/project/pallas_call | solution.py:89
  62.8 21.3 %attend_forward.1 = (bf16[1024,768]{1,0:T(8,128)(2,1)S(1)}, f32[6,1024,128]{2,1,0:T(8,128)S(1)}) custom-call(s32[1024,1]{1,0:T(8,128)S(1)} %copy.59.col_ref.seg_ref, s32[1,1024]{1,0:T(1,128)S(1)} %bitcast.111, bf16[3,1024,768]{2,1,0:T(8,128)(2,1)S(1)} %get-tuple-element.43.qkv_ref), custom_call_target="tpu_custom_call" | custom-call | flops 12884901888 | bytes 9437184 | tf_op jit(solution)/shard_map/attend_forward/pallas_call | solution.py:150
  92.1 3.7 middle.1
  101.0 11.6 %all-gather.14.cloned.1.call-done = bf16[12288,128]{1,0:T(8,128)(2,1)} async-done(((bf16[1536,128]{1,0:T(8,128)(2,1)}), bf16[12288,128]{1,0:T(8,128)(2,1)}) %all-gather.14.cloned.1.call-update) | async-done | bytes 3145744 | tf_op jit(solution)/shard_map/all_gather | solution.py:650
  116.9 17.5 %feed.3 = (f32[1024,768]{1,0:T(8,128)}, f32[1024,768]{1,0:T(8,128)}, bf16[8,1536,128]{2,1,0:T(8,128)(2,1)}, f32[1,1024]{1,0:T(1,128)S(1)}) custom-call(s32[1]{0:T(128)} %constant.1.clone.1.order_ref, bf16[8,1536,128]{2,1,0:T(8,128)(2,1)} %bitcast.158, bf16[1024,768]{1,0:T(8,128)(2,1)S(1)} %copy-done.19, bf16[768,1024]{1,0:T(8,128)(2,1)S(1)} %copy-done.23, ...), custom_call_target="tpu_custom_call" | custom-call | flops 9663676416 | bytes 15728640 | tf_op jit(solution)/shard_map/feed/pallas_call | solution.py:387
  134.3 13.0 %all-gather.12.cloned.1.call-done = bf16[12288,128]{1,0:T(8,128)(2,1)} async-done(((bf16[1536,128]{1,0:T(8,128)(2,1)}), bf16[12288,128]{1,0:T(8,128)(2,1)}) %all-gather.12.cloned.1.call-update) | async-done | bytes 3145744 | tf_op jit(solution)/shard_map/all_gather | solution.py:650
  151.5 18.1 %feed.4 = (f32[1024,768]{1,0:T(8,128)}, f32[1024,768]{1,0:T(8,128)}, bf16[8,1536,128]{2,1,0:T(8,128)(2,1)}, f32[1,1024]{1,0:T(1,128)S(1)}) custom-call(s32[1]{0:T(128)} %constant.1.clone.1.order_ref, bf16[8,1536,128]{2,1,0:T(8,128)(2,1)} %bitcast.159, bf16[1024,768]{1,0:T(8,128)(2,1)S(1)} %copy-done.20, bf16[768,1024]{1,0:T(8,128)(2,1)S(1)} %copy-done.24, ...), custom_call_target="tpu_custom_call" | custom-call | flops 9663676416 | bytes 15728640 | tf_op jit(solution)/shard_map/feed/pallas_call | solution.py:387
  169.6 12.4 %all-gather.8.cloned.1.call-done = bf16[12288,128]{1,0:T(8,128)(2,1)} async-done(((bf16[1536,128]{1,0:T(8,128)(2,1)}), bf16[12288,128]{1,0:T(8,128)(2,1)}) %all-gather.8.cloned.1.call-update) | async-done | bytes 3145744 | tf_op jit(solution)/shard_map/all_gather | solution.py:650
  186.2 18.2 %feed.5 = (f32[1024,768]{1,0:T(8,128)}, f32[1024,768]{1,0:T(8,128)}, bf16[8,1536,128]{2,1,0:T(8,128)(2,1)}, f32[1,1024]{1,0:T(1,128)S(1)}) custom-call(s32[1]{0:T(128)} %constant.1.clone.1.order_ref, bf16[8,1536,128]{2,1,0:T(8,128)(2,1)} %bitcast.160, bf16[1024,768]{1,0:T(8,128)(2,1)S(1)} %copy-done.21, bf16[768,1024]{1,0:T(8,128)(2,1)S(1)} %copy-done.25, ...), custom_call_target="tpu_custom_call" | custom-call | flops 9663676416 | bytes 15728640 | tf_op jit(solution)/shard_map/feed/pallas_call | solution.py:387
  206.3 9.1 %branch.1 = (bf16[1024,768]{1,0:T(8,128)(2,1)}, f32[1024,768]{1,0:T(8,128)S(1)}, bf16[1024,768]{1,0:T(8,128)(2,1)S(1)}, bf16[8,576,128]{2,1,0:T(8,128)(2,1)}, f32[8,768]{1,0:T(8,128)S(1)}) custom-call(s32[1]{0:T(128)} %constant.1.clone.1.order_ref, bf16[8,576,128]{2,1,0:T(8,128)(2,1)S(1)} %bitcast.108, f32[1024,768]{1,0:T(8,128)S(1)} %copy-done.3, ...), custom_call_target="tpu_custom_call" | custom-call | flops 2415919104 | bytes 18874368 | tf_op jit(solution)/shard_map/branch/pallas_call | solution.py:466
  221.7 29.0 %attend_backward.1.grads_ref.grad_ref = bf16[3,1024,768]{2,1,0:T(8,128)(2,1)S(1)} custom-call(s32[1024,1]{1,0:T(8,128)S(1)} %copy.59.col_ref.seg_ref, s32[1,1024]{1,0:T(1,128)S(1)} %bitcast.112, bf16[3,1024,768]{2,1,0:T(8,128)(2,1)} %copy-done.30, bf16[1024,768]{1,0:T(8,128)(2,1)S(1)} %get-tuple-element.44.mixed_ref, f32[6,1024,128]{2,1,0:T(8,128)S(1)} %copy-done.34, ...), custom_call_target="tpu_custom_call" | custom-call | flops 32212254720 | bytes 15728640 | tf_op jit(solution)/shard_map/attend_backward/pallas_call | solution.py:245
  250.7 7.6 %triple_grad.1 = (bf16[8,1728,128]{2,1,0:T(8,128)(2,1)}, f32[1,2304]{1,0:T(1,128)S(1)}) custom-call(s32[1]{0:T(128)} %constant.1.clone.1.order_ref, bf16[768,1024]{1,0:T(8,128)(2,1)S(1)} %copy-done.32, bf16[3,1024,768]{2,1,0:T(8,128)(2,1)S(1)} %attend_backward.1.grads_ref.grad_ref), custom_call_target="tpu_custom_call" | custom-call | flops 3623878656 | bytes 9437184 | tf_op jit(solution)/shard_map/triple_grad/pallas_call | solution.py:519
  263.3 2.2 copy-done.17
  265.5 2.8 copy-done.29
  268.3 7.4 %input_grad.1 = (bf16[1024,768]{1,0:T(8,128)(2,1)}, f32[8,768]{1,0:T(8,128)S(1)}) custom-call(s32[1]{0:T(128)} %constant.1.clone.1.order_ref, bf16[8,1744,128]{2,1,0:T(8,128)(2,1)S(1)} %bitcast.118, bf16[1024,768]{1,0:T(8,128)(2,1)S(1)} %copy-done.12, bf16[3,1024,768]{2,1,0:T(8,128)(2,1)S(1)} %copy-done.29, f32[1024,768]{1,0:T(8,128)S(1)} %copy-done.17, ...), custom_call_target="tpu_custom_call" | custom-call | flops 3623878656 | bytes 14155776 | tf_op jit(solution)/shard_map/input_grad/pallas_call | solution.py:560
  278.8 28.5 %reduce-scatter.9.cloned.1.call-done = bf16[1728,128]{1,0:T(8,128)(2,1)} async-done(((bf16[13824,128]{1,0:T(8,128)(2,1)}), bf16[1728,128]{1,0:T(8,128)(2,1)}) %reduce-scatter.9.cloned.1.call-update) | async-done | bytes 442384 | tf_op jit(solution)/shard_map/reduce_scatter | solution.py:595
  309.1 48.2 %reduce-scatter.17.cloned.1.call-done = bf16[1536,128]{1,0:T(8,128)(2,1)} async-done(((bf16[12288,128]{1,0:T(8,128)(2,1)}), bf16[1536,128]{1,0:T(8,128)(2,1)}) %reduce-scatter.17.cloned.1.call-update) | async-done | bytes 393232 | tf_op jit(solution)/shard_map/reduce_scatter | solution.py:595
  357.3 49.6 %reduce-scatter.15.cloned.1.call-done = bf16[1536,128]{1,0:T(8,128)(2,1)} async-done(((bf16[12288,128]{1,0:T(8,128)(2,1)}), bf16[1536,128]{1,0:T(8,128)(2,1)}) %reduce-scatter.15.cloned.1.call-update) | async-done | bytes 393232 | tf_op jit(solution)/shard_map/reduce_scatter | solution.py:595
  406.9 49.9 %reduce-scatter.13.cloned.1.call-done = bf16[1536,128]{1,0:T(8,128)(2,1)} async-done(((bf16[12288,128]{1,0:T(8,128)(2,1)}), bf16[1536,128]{1,0:T(8,128)(2,1)}) %reduce-scatter.13.cloned.1.call-update) | async-done | bytes 393232 | tf_op jit(solution)/shard_map/reduce_scatter | solution.py:595
  456.8 34.9 %reduce-scatter.7.cloned.1.call-done = bf16[16,128]{1,0:T(8,128)(2,1)} async-done(((bf16[128,128]{1,0:T(8,128)(2,1)}), bf16[16,128]{1,0:T(8,128)(2,1)}) %reduce-scatter.7.cloned.1.call-update) | async-done | bytes 4112 | tf_op jit(solution)/shard_map/reduce_scatter | solution.py:595
  491.7 11.8 %psum.42 = bf16[2048]{0:T(1024)(128)(2,1)S(1)} all-reduce(bf16[2048]{0:T(1024)(128)(2,1)} %bitcast.157), channel_id=1, replica_groups=mesh['shard'=8,'rep'=4] {'rep'}, use_global_device_ids=true, to_apply=%region_1.2 | all-reduce | flops 2048 | bytes 8192 | tf_op jit(solution)/shard_map/psum | solution.py:595
  505.4 67.0 %all-reduce.5.cloned.1.call-done = (bf16[96,2304]{1,0:T(8,128)(2,1)}, bf16[96,768]{1,0:T(8,128)(2,1)}, bf16[1536,128]{1,0:T(8,128)(2,1)}, bf16[1536,128]{1,0:T(8,128)(2,1)}, bf16[1536,128]{1,0:T(8,128)(2,1)}) async-done(((bf16[96,2304]{1,0:T(8,128)(2,1)}, bf16[96,768]{1,0:T(8,128)(2,1)}, bf16[1536,128]{1,0:T(8,128)(2,1)}, bf16[1536,128]{1,0:T(8,128)(2,1)}, bf16[1536,128]{1,0:T(8,128)(2,1)}), ...) | async-done | bytes 1769488 | tf_op jit(solution)/shard_map/psum | solution.py:595
  (185 shorter events, 67.8 us)
Async XLA Ops:
  7.2 44.7 %all-gather.10.cloned.1.call-start = ((), (), s32[]{:S(2)}) async-start(), calls=%async_computation.8 | async-start | bytes 4018176 | tf_op jit(solution)/shard_map/all_gather | solution.py:650
  12.7 2.3 copy-start.40
  14.9 73.0 %all-gather.6.cloned.1.call-start = ((), (), s32[]{:S(2)}) async-start(), calls=%async_computation.6 | async-start | bytes 1327104 | tf_op jit(solution)/shard_map/all_gather | solution.py:650
  15.8 96.8 %all-gather.14.cloned.1.call-start = ((), (), s32[]{:S(2)}) async-start(), calls=%async_computation.10 | async-start | bytes 3538944 | tf_op jit(solution)/shard_map/all_gather | solution.py:650
  18.9 128.4 %all-gather.12.cloned.1.call-start = ((), (), s32[]{:S(2)}) async-start(), calls=%async_computation.9 | async-start | bytes 3538944 | tf_op jit(solution)/shard_map/all_gather | solution.py:650
  20.2 161.8 %all-gather.8.cloned.1.call-start = ((), (), s32[]{:S(2)}) async-start(), calls=%async_computation.7 | async-start | bytes 3538944 | tf_op jit(solution)/shard_map/all_gather | solution.py:650
  20.4 33.0 %copy-start.10 = (bf16[1024,768]{1,0:T(8,128)(2,1)S(1)}, bf16[1024,768]{1,0:T(8,128)(2,1)}, u32[]{:S(2)}) copy-start(bf16[1024,768]{1,0:T(8,128)(2,1)} %x_ref.5) | copy-start | bytes 4718596
  21.5 255.7 %reduce-scatter.11.cloned.1.call-start = ((), (), s32[]{:S(2)}) async-start(), calls=%async_computation.13 | async-start | bytes 1327104 | tf_op jit(solution)/shard_map/reduce_scatter | solution.py:595
  84.1 2.1 copy-start.30
  186.2 18.2 %copy-start.1 = (bf16[4608,128]{1,0:T(8,128)(2,1)S(1)}, bf16[4608,128]{1,0:T(8,128)(2,1)}, u32[]{:S(2)}) copy-start(bf16[4608,128]{1,0:T(8,128)(2,1)} %all-gather.6.cloned.1.call-done) | copy-start | bytes 3538948
  186.2 18.2 %copy-start.8 = (bf16[1024,768]{1,0:T(8,128)(2,1)S(1)}, bf16[1024,768]{1,0:T(8,128)(2,1)}, u32[]{:S(2)}) copy-start(bf16[1024,768]{1,0:T(8,128)(2,1)} %copy-done.4) | copy-start | bytes 4718596
  218.3 89.0 %reduce-scatter.9.cloned.1.call-start = ((), (), s32[]{:S(2)}) async-start(), calls=%async_computation.12 | async-start | bytes 3981312 | tf_op jit(solution)/shard_map/reduce_scatter | solution.py:595
  221.6 29.0 %copy-start.32 = (bf16[768,1024]{1,0:T(8,128)(2,1)S(1)}, bf16[768,1024]{1,0:T(8,128)(2,1)}, u32[]{:S(2)}) copy-start(bf16[768,1024]{1,0:T(8,128)(2,1)} %copy-done.31) | copy-start | bytes 4718596
  250.7 7.6 %copy-start.28 = (bf16[3,1024,768]{2,1,0:T(8,128)(2,1)}, bf16[3,1024,768]{2,1,0:T(8,128)(2,1)S(1)}, u32[]{:S(2)}) copy-start(bf16[3,1024,768]{2,1,0:T(8,128)(2,1)S(1)} %attend_backward.1.grads_ref.grad_ref) | copy-start | bytes 14155780
  258.3 99.0 %reduce-scatter.17.cloned.1.call-start = ((), (), s32[]{:S(2)}) async-start(), calls=%async_computation.16 | async-start | bytes 3538944 | tf_op jit(solution)/shard_map/reduce_scatter | solution.py:595
  259.1 147.9 %reduce-scatter.15.cloned.1.call-start = ((), (), s32[]{:S(2)}) async-start(), calls=%async_computation.15 | async-start | bytes 3538944 | tf_op jit(solution)/shard_map/reduce_scatter | solution.py:595
  259.8 197.0 %reduce-scatter.13.cloned.1.call-start = ((), (), s32[]{:S(2)}) async-start(), calls=%async_computation.14 | async-start | bytes 3538944 | tf_op jit(solution)/shard_map/reduce_scatter | solution.py:595
  260.4 231.3 %reduce-scatter.7.cloned.1.call-start = ((), (), s32[]{:S(2)}) async-start(), calls=%async_computation.11 | async-start | bytes 36864 | tf_op jit(solution)/shard_map/reduce_scatter | solution.py:595
  263.3 2.2 copy-start.17
  265.5 2.8 copy-start.29
  277.1 295.2 %all-reduce.5.cloned.1.call-start = ((), (), s32[]{:S(2)}) async-start(), calls=%async_computation.17 | async-start | bytes 3538944 | tf_op jit(solution)/shard_map/psum | solution.py:595
  572.4 3.1 copy-start.37
  572.4 4.0 copy-start.38
  572.4 4.0 copy-start.39
  (29 other events, 43.2 us)
Sparse Core Ops, SparseCore 0:
  15.0 36.7 all-gather.9
  54.3 24.0 all-gather.5
  80.3 32.3 all-gather.13
  114.9 32.3 all-gather.11
  149.6 32.3 all-gather.7
  218.4 36.7 reduce-scatter.10
  259.1 48.1 reduce-scatter.8
  311.0 46.2 reduce-scatter.16
  360.7 46.2 reduce-scatter.14
  410.5 46.2 reduce-scatter.12
  460.4 31.2 reduce-scatter.6
  495.1 77.1 all-reduce.4
